TPU v7x, 256 devices: a whole 4x4x8 slice. The times are simulated.
256 devices in a mesh: dp: 4 (over y_lo, core), fsdp: 64 (over z, y_hi, x).
Axes of the slice: x: 4, y: 4 (y_hi: 2, y_lo: 2; y = y_hi * 2 + y_lo), z: 8, core: 2. Of those that a mesh axis runs over, the one named last changes fastest.
Arguments:
- tokens: bfloat16 [1024, 5120], P('dp', 'fsdp'), may hold values from -6 to 6
- cotangent: bfloat16 [1024, 5120], P('dp', 'fsdp'), may hold values from -6 to 6
- pass_counts: int32 [64], replicated, may hold values from 0 to 8
- group_ids: int32 [64], replicated, may hold values from 0 to 7
- token_rollout: int32 [1024], P('dp'), may hold values from 0 to 63, never falling along the last dimension, each value on 1 to 32 neighbouring positions
- master_gate: float32 [13824, 5120], P('fsdp', 'dp'), may hold values from -0.078125 to 0.078125
- master_up: float32 [13824, 5120], P('fsdp', 'dp'), may hold values from -0.078125 to 0.078125
- master_down: float32 [13824, 5120], P('fsdp', 'dp'), may hold values from -0.0546875 to 0.0546875
- moment_gate: float32 [13824, 5120], P('fsdp', 'dp'), may hold values from -12 to 12
- moment_up: float32 [13824, 5120], P('fsdp', 'dp'), may hold values from -12 to 12
- moment_down: float32 [13824, 5120], P('fsdp', 'dp'), may hold values from -12 to 12
- second_gate: float32 [13824, 5120], P('fsdp', 'dp'), may hold values from 4 to 400
- second_up: float32 [13824, 5120], P('fsdp', 'dp'), may hold values from 4 to 400
- second_down: float32 [13824, 5120], P('fsdp', 'dp'), may hold values from 4 to 400
Outputs:
- block_out: bfloat16 [1024, 5120], P('dp', 'fsdp')
- grad_input: bfloat16 [1024, 5120], P('dp', 'fsdp')
- update_gate: bfloat16 [13824, 5120], P('fsdp', 'dp')
- update_up: bfloat16 [13824, 5120], P('fsdp', 'dp')
- update_down: bfloat16 [13824, 5120], P('fsdp', 'dp')
Inputs may be any that keep to these rules, and one draw needn't show every extreme that they name: `token_rollout`: tokens of one rollout are consecutive, rollout numbers never fall along the tokens, and every rollout has at least one token.
All inputs are finite; a program needn't handle non-finite values.
Results may differ from a plain program's by a relative error of at most 0.008.
Values may be sent and summed in bfloat16 or wider, within the bound.
A program may use at most 128 MiB of HBM per device.

v0:
```python
import jax
import jax.numpy as jnp
from jax import lax
from jax.sharding import PartitionSpec as P

ROLL = 64
TESTS = 8


beta_first = 0.9
beta_second = 0.95
adam_epsilon = 1e-08
weight_decay = 0.1
correct_first = 1.0 - 0.9**10
correct_second = 1.0 - 0.95**10


def contract(left_op, right_op, left_dim, right_dim):
    return lax.dot_general(
        left_op,
        right_op,
        (((left_dim,), (right_dim,)), ((), ())),
        preferred_element_type=jnp.float32,
    )


def adamw(master, moment, second, gradient):
    moment_new = beta_first * moment + (1.0 - beta_first) * gradient
    second_new = beta_second * second + (1.0 - beta_second) * gradient * gradient
    result = (
        moment_new / correct_first / (jnp.sqrt(second_new / correct_second) + adam_epsilon)
        + weight_decay * master
    )
    return result.astype(jnp.bfloat16)


def body(
    tokens,
    cotangent,
    pass_counts,
    group_ids,
    token_rollout,
    master_gate,
    master_up,
    master_down,
    moment_gate,
    moment_up,
    moment_down,
    second_gate,
    second_up,
    second_down,
):
    reward = pass_counts.astype(jnp.float32) / TESTS
    same_group = (group_ids[:, None] == group_ids[None, :]).astype(jnp.float32)
    baseline = jnp.sum(same_group * reward[None, :], axis=1) / jnp.sum(same_group, axis=1)
    advantage = reward - baseline
    picker = (token_rollout[:, None] == jnp.arange(ROLL, dtype=jnp.int32)[None, :]).astype(
        jnp.float32
    )
    token_adv = jnp.sum(picker * advantage[None, :], axis=1)
    gathered = lax.all_gather(tokens, "fsdp", axis=1, tiled=True)
    w_gate, w_up, w_down = (
        lax.all_gather(master_gate.astype(jnp.bfloat16), "dp", axis=1, tiled=True),
        lax.all_gather(master_up.astype(jnp.bfloat16), "dp", axis=1, tiled=True),
        lax.all_gather(master_down.astype(jnp.bfloat16), "dp", axis=1, tiled=True),
    )
    gate_in = contract(gathered, w_gate, 1, 1)
    up_in = contract(gathered, w_up, 1, 1)
    sigmoid_v = jax.nn.sigmoid(gate_in)
    active = gate_in * sigmoid_v
    slopes = sigmoid_v * (1.0 + gate_in * (1.0 - sigmoid_v))
    hidden = (active * up_in).astype(jnp.bfloat16)
    partial_out = jnp.dot(hidden, w_down, preferred_element_type=jnp.float32)
    block_out = lax.psum_scatter(partial_out, "fsdp", scatter_dimension=1, tiled=True).astype(
        jnp.bfloat16
    )
    upstream = lax.all_gather(cotangent, "fsdp", axis=1, tiled=True)
    delta_out = (-token_adv[:, None] * upstream.astype(jnp.float32)).astype(jnp.bfloat16)
    d_hidden = contract(delta_out, w_down, 1, 1)
    d_gate = (d_hidden * up_in * slopes).astype(jnp.bfloat16)
    d_up = (d_hidden * active).astype(jnp.bfloat16)
    partial_input = jnp.dot(d_gate, w_gate, preferred_element_type=jnp.float32) + jnp.dot(
        d_up, w_up, preferred_element_type=jnp.float32
    )
    grad_input = lax.psum_scatter(partial_input, "fsdp", scatter_dimension=1, tiled=True).astype(
        jnp.bfloat16
    )
    grad_gate, grad_up, grad_down = (
        lax.psum_scatter(contract(d_gate, gathered, 0, 0), "dp", scatter_dimension=1, tiled=True),
        lax.psum_scatter(contract(d_up, gathered, 0, 0), "dp", scatter_dimension=1, tiled=True),
        lax.psum_scatter(contract(hidden, delta_out, 0, 0), "dp", scatter_dimension=1, tiled=True),
    )
    update_gate = adamw(master_gate, moment_gate, second_gate, grad_gate)
    update_up = adamw(master_up, moment_up, second_up, grad_up)
    update_down = adamw(master_down, moment_down, second_down, grad_down)
    return (block_out, grad_input, update_gate, update_up, update_down)


def solution(mesh):
    in_specs = (
        P("dp", "fsdp"),
        P("dp", "fsdp"),
        P(),
        P(),
        P("dp"),
        P("fsdp", "dp"),
        P("fsdp", "dp"),
        P("fsdp", "dp"),
        P("fsdp", "dp"),
        P("fsdp", "dp"),
        P("fsdp", "dp"),
        P("fsdp", "dp"),
        P("fsdp", "dp"),
        P("fsdp", "dp"),
    )
    out_specs = (
        P("dp", "fsdp"),
        P("dp", "fsdp"),
        P("fsdp", "dp"),
        P("fsdp", "dp"),
        P("fsdp", "dp"),
    )
    return jax.shard_map(body, mesh=mesh, in_specs=in_specs, out_specs=out_specs, check_vma=False)
```

profile of v0, /device:TPU:8, one launch (start us, length us, event | category | flops | bytes accessed | tf_op | source)
XLA Modules:
  0.0 1280.8 jit_solution(13808638514191233851)
XLA Ops:
  7.2 2.2 convert_element_type.46
  12.1 32.1 %all-gather.8.cloned.1.call-done = bf16[216,5120]{1,0:T(8,128)(2,1)} async-done(((bf16[216,1280]{1,0:T(8,128)(2,1)}), bf16[216,5120]{1,0:T(8,128)(2,1)}) %all-gather.8.cloned.1.call-update) | async-done | bytes 2211856 | tf_op jit(solution)/shard_map/all_gather | solution.py:63
  44.2 125.9 %all-gather.6.cloned.1.call-done = bf16[256,5120]{0,1:T(8,128)(2,1)} async-done(((bf16[256,80]{0,1:T(8,128)(2,1)}), bf16[256,5120]{0,1:T(8,128)(2,1)}) %all-gather.6.cloned.1.call-update) | async-done | bytes 2621456 | tf_op jit(solution)/shard_map/all_gather | solution.py:61
  170.1 3.3 fusion.26
  173.4 27.4 %all-gather.10.cloned.1.call-done = bf16[216,5120]{1,0:T(8,128)(2,1)} async-done(((bf16[216,1280]{1,0:T(8,128)(2,1)}), bf16[216,5120]{1,0:T(8,128)(2,1)}) %all-gather.10.cloned.1.call-update) | async-done | bytes 2211856 | tf_op jit(solution)/shard_map/all_gather | solution.py:64
  200.8 2.4 multiply_convert_fusion.5
  203.2 123.4 %all-gather.14.cloned.1.call-done = bf16[256,5120]{0,1:T(8,128)(2,1)} async-done(((bf16[256,80]{0,1:T(8,128)(2,1)}), bf16[256,5120]{0,1:T(8,128)(2,1)}) %all-gather.14.cloned.1.call-update) | async-done | bytes 2621456 | tf_op jit(solution)/shard_map/all_gather | solution.py:77
  326.6 4.8 fusion
  331.4 45.6 %reduce-scatter.14.cloned.1.call-done = f32[216,1280]{1,0:T(8,128)} async-done(((f32[216,5120]{1,0:T(8,128)}), f32[216,1280]{1,0:T(8,128)}) %reduce-scatter.14.cloned.1.call-update) | async-done | bytes 1105936 | tf_op jit(solution)/shard_map/reduce_scatter | solution.py:91
  377.0 4.3 fusion.20
  381.4 33.7 %all-gather.12.cloned.1.call-done = bf16[216,5120]{1,0:T(8,128)(2,1)} async-done(((bf16[216,1280]{1,0:T(8,128)(2,1)}), bf16[216,5120]{1,0:T(8,128)(2,1)}) %all-gather.12.cloned.1.call-update) | async-done | bytes 2211856 | tf_op jit(solution)/shard_map/all_gather | solution.py:65
  415.1 3.2 multiply_convert_fusion.3
  418.3 3.0 fusion.30
  421.4 3.1 fusion.29
  424.5 1.5 copy-done.6
  426.1 3.5 fusion.27
  429.7 1.5 copy-done.1
  432.8 3.7 convolution_add_fusion
  436.6 35.6 %reduce-scatter.12.cloned.1.call-done = f32[216,1280]{1,0:T(8,128)} async-done(((f32[216,5120]{1,0:T(8,128)}), f32[216,1280]{1,0:T(8,128)}) %reduce-scatter.12.cloned.1.call-update) | async-done | bytes 1105936 | tf_op jit(solution)/shard_map/reduce_scatter | solution.py:90
  472.2 3.2 fusion.21
  475.4 50.2 %reduce-scatter.10.cloned.1.call-done = f32[216,1280]{1,0:T(8,128)} async-done(((f32[216,5120]{1,0:T(8,128)}), f32[216,1280]{1,0:T(8,128)}) %reduce-scatter.10.cloned.1.call-update) | async-done | bytes 1105936 | tf_op jit(solution)/shard_map/reduce_scatter | solution.py:89
  525.6 3.5 fusion.22
  529.1 373.9 %reduce-scatter.6.cloned.1.call-done = f32[256,80]{0,1:T(8,128)} async-done(((f32[256,5120]{0,1:T(8,128)}), f32[256,80]{0,1:T(8,128)}) %reduce-scatter.6.cloned.1.call-update) | async-done | bytes 81936 | tf_op jit(solution)/shard_map/reduce_scatter | solution.py:74
  904.6 367.9 %reduce-scatter.8.cloned.1.call-done = f32[256,80]{0,1:T(8,128)} async-done(((f32[256,5120]{0,1:T(8,128)}), f32[256,80]{0,1:T(8,128)}) %reduce-scatter.8.cloned.1.call-update) | async-done | bytes 81936 | tf_op jit(solution)/shard_map/reduce_scatter | solution.py:85
  (49 shorter events, 7.6 us)
Async XLA Ops:
  7.2 3.1 copy-start.2
  7.2 37.0 %all-gather.8.cloned.1.call-start = ((), (), s32[]{:S(2)}) async-start(), calls=%async_computation.6 | async-start | bytes 2764800 | tf_op jit(solution)/shard_map/all_gather | solution.py:63
  9.4 160.7 %all-gather.6.cloned.1.call-start = ((), (), s32[]{:S(2)}) async-start(), calls=%async_computation.5 | async-start | bytes 2662400 | tf_op jit(solution)/shard_map/all_gather | solution.py:61
  10.2 1.6 copy-start.10
  10.2 1.6 copy-start.8
  10.2 1.8 copy-start.9
  10.2 190.6 %all-gather.10.cloned.1.call-start = ((), (), s32[]{:S(2)}) async-start(), calls=%async_computation.7 | async-start | bytes 2764800 | tf_op jit(solution)/shard_map/all_gather | solution.py:64
  11.2 315.4 %all-gather.14.cloned.1.call-start = ((), (), s32[]{:S(2)}) async-start(), calls=%async_computation.10 | async-start | bytes 2662400 | tf_op jit(solution)/shard_map/all_gather | solution.py:77
  11.7 365.3 %reduce-scatter.14.cloned.1.call-start = ((), (), s32[]{:S(2)}) async-start(), calls=%async_computation.14 | async-start | bytes 5529600 | tf_op jit(solution)/shard_map/reduce_scatter | solution.py:91
  170.1 30.7 %copy-start = (bf16[256,5120]{0,1:T(8,128)(2,1)S(1)}, bf16[256,5120]{0,1:T(8,128)(2,1)}, u32[]{:S(2)}) copy-start(bf16[256,5120]{0,1:T(8,128)(2,1)} %all-gather.6.cloned.1.call-done) | copy-start | bytes 7864324
  331.4 83.7 %all-gather.12.cloned.1.call-start = ((), (), s32[]{:S(2)}) async-start(), calls=%async_computation.8 | async-start | bytes 2764800 | tf_op jit(solution)/shard_map/all_gather | solution.py:65
  381.4 90.8 %reduce-scatter.12.cloned.1.call-start = ((), (), s32[]{:S(2)}) async-start(), calls=%async_computation.13 | async-start | bytes 5529600 | tf_op jit(solution)/shard_map/reduce_scatter | solution.py:90
  421.3 104.3 %reduce-scatter.10.cloned.1.call-start = ((), (), s32[]{:S(2)}) async-start(), calls=%async_computation.12 | async-start | bytes 5529600 | tf_op jit(solution)/shard_map/reduce_scatter | solution.py:89
  424.5 1.6 copy-start.6
  424.5 478.6 %reduce-scatter.6.cloned.1.call-start = ((), (), s32[]{:S(2)}) async-start(), calls=%async_computation.9 | async-start | bytes 5324800 | tf_op jit(solution)/shard_map/reduce_scatter | solution.py:74
  429.6 1.6 copy-start.1
  429.6 842.9 %reduce-scatter.8.cloned.1.call-start = ((), (), s32[]{:S(2)}) async-start(), calls=%async_computation.11 | async-start | bytes 5324800 | tf_op jit(solution)/shard_map/reduce_scatter | solution.py:85
  431.2 1.6 copy-start.5
  436.6 35.6 %copy-start.3 = (f32[216,1280]{1,0:T(8,128)S(1)}, f32[216,1280]{1,0:T(8,128)}, u32[]{:S(2)}) copy-start(f32[216,1280]{1,0:T(8,128)} %param.20) | copy-start | bytes 3317764
  436.6 35.6 %copy-start.7 = (f32[216,1280]{1,0:T(8,128)S(1)}, f32[216,1280]{1,0:T(8,128)}, u32[]{:S(2)}) copy-start(f32[216,1280]{1,0:T(8,128)} %param.26) | copy-start | bytes 3317764
  436.6 89.0 %copy-start.4 = (f32[216,1280]{1,0:T(8,128)S(1)}, f32[216,1280]{1,0:T(8,128)}, u32[]{:S(2)}) copy-start(f32[216,1280]{1,0:T(8,128)} %param.19) | copy-start | bytes 3317764
Sparse Core Ops, SparseCore 0:
  10.4 33.7 all-gather.7
  47.8 122.2 all-gather.5
  172.5 28.2 all-gather.9
  204.3 122.2 all-gather.13
  331.5 45.4 reduce-scatter.13
  381.5 33.5 all-gather.11
  421.4 50.7 reduce-scatter.11
  474.8 50.7 reduce-scatter.9
  528.3 374.7 reduce-scatter.5
  905.6 366.8 reduce-scatter.7
where the time goes:
time: 1280 us
  waiting for transfers between devices  1220 us (95%)
  matrix products  28.1 us (2%)
  other arithmetic  17.4 us (1%)
  between operations  14.3 us (1%)
    reduce_scatter x1, waiting for transfers between devices, body(): lax.psum_scatter(partial_out, 'fsdp', scatter_dimension=1, tiled=True)  374 us
    reduce_scatter x1, waiting for transfers between devices, body(): lax.psum_scatter(partial_input, 'fsdp', scatter_dimension=1, tiled=True)  368 us
    all_gather x1, waiting for transfers between devices, body(): gathered = lax.all_gather(tokens, 'fsdp', axis=1, tiled=True)  126 us
    all_gather x1, waiting for transfers between devices, body(): upstream = lax.all_gather(cotangent, 'fsdp', axis=1, tiled=True)  123 us
    reduce_scatter x1, waiting for transfers between devices, body(): lax.psum_scatter(contract(d_gate, gathered, 0, 0), 'dp', scatter_dimensio...  50.2 us
    reduce_scatter x1, waiting for transfers between devices, body(): lax.psum_scatter(contract(hidden, delta_out, 0, 0), 'dp', scatter_dimensi...  45.6 us
    reduce_scatter x1, waiting for transfers between devices, body(): lax.psum_scatter(contract(d_up, gathered, 0, 0), 'dp', scatter_dimension=...  35.6 us
    all_gather x1, waiting for transfers between devices, body(): lax.all_gather(master_down.astype(jnp.bfloat16), 'dp', axis=1, tiled=True)  33.7 us
  transfers between devices with their start and end apart: 10, of which 10 were waited for; matrix products, arithmetic and copies ran while one was open for 2% of the time, Pallas kernels for 0%

commit v1 on v0

v1 whole, which is shorter than its diff:
```python
import jax
import jax.numpy as jnp
from jax import lax
from jax.experimental import pallas as pl
from jax.experimental.pallas import tpu as pltpu
from jax.sharding import PartitionSpec as P

ROLL = 64
TESTS = 8
beta_first = 0.9
beta_second = 0.95
adam_epsilon = 1e-08
weight_decay = 0.1
correct_first = 1.0 - 0.9**10
correct_second = 1.0 - 0.95**10

FFS = 216
PAD = 224
HID = 256
DS = 1280
FB = 80
TB = 256
F32 = jnp.float32
BF16 = jnp.bfloat16


def rem(a, b):
    return lax.rem(a, jnp.int32(b))


def div(a, b):
    return lax.div(a, jnp.int32(b))


def remote(src, dst, send, recv, device):
    return pltpu.make_async_remote_copy(
        src_ref=src,
        dst_ref=dst,
        send_sem=send,
        recv_sem=recv,
        device_id=device,
        device_id_type=pl.DeviceIdType.MESH,
    )


def kernel(
    tok, dlt, mg, mu, md, og, ou, od, sg, su, sd,
    bo, gi, ug, uu, ud,
    XT, PO, RXO, RXR, RXC, ZR, YS, YR, FS, FR,
    MW, MOM, SEC, WB, WT, HD, DG, DU, GUO, ACT, US, DHO,
    SD, RD, SY, RY, SD2, RD2, SY2, RY2, GR, UO0, UO1, UO2,
    lsem, p_s, p_r, y_s, y_r, z_s, z_r, xr_s, xr_r, xl_s, xl_r, f_s, f_r,
    o_s, o_r, w_s, w_r, c_s, c_r, zz_s, zz_r, yy_s, yy_r, pp_s, pp_r,
    d_s, d_r, e_s, e_r,
):
    dp = lax.axis_index("dp")
    fs = lax.axis_index("fsdp")
    z, yh, x = div(fs, 8), rem(div(fs, 4), 2), rem(fs, 4)
    core = rem(dp, 2)
    right, left, far = rem(x + 1, 4), rem(x + 3, 4), rem(x + 2, 4)

    def at(dp_, z_, y_, x_):
        return (dp_, z_ * 8 + y_ * 4 + x_)

    d_right, d_left = at(dp, z, yh, right), at(dp, z, yh, left)
    d_y = at(dp, z, 1 - yh, x)
    home = div(z, 2)
    zq = 2 * dp + rem(z, 2)
    d_p = at(home, zq, yh, x)
    d_core = at(dp + 1 - 2 * core, z, yh, x)
    d_chip = at(rem(dp + 2, 4), z, yh, x)
    at_home = home == dp

    srcs = (mg, mu, md, og, ou, od, sg, su, sd)
    loads = []
    for n, src in enumerate(srcs):
        dst = (MW, MOM, SEC)[n // 3].at[n % 3, pl.ds(0, FFS)]
        loads.append(pltpu.make_async_copy(src, dst, lsem.at[n]))
    for load in loads:
        load.start()

    for w in range(3):
        MW[w, FFS:HID, :] = jnp.zeros((HID - FFS, DS), F32)
    for buf in (HD, DG, DU):
        for n in range(4):
            buf[n, PAD:HID, :] = jnp.zeros((HID - PAD, TB), BF16)

    barrier = pltpu.get_barrier_semaphore()
    for peer in (d_right, d_left, d_y, d_core, d_chip):
        pl.semaphore_signal(barrier, inc=1, device_id=peer, device_id_type=pl.DeviceIdType.MESH)

    @pl.loop(1, 8)
    def _(d):
        pl.semaphore_signal(
            barrier, inc=1, device_id=at(dp, rem(z + d, 8), yh, x), device_id_type=pl.DeviceIdType.MESH
        )

    @pl.when(jnp.logical_not(at_home))
    def _():
        pl.semaphore_signal(barrier, inc=1, device_id=d_p, device_id_type=pl.DeviceIdType.MESH)
        pl.semaphore_wait(barrier, 13)

    @pl.when(at_home)
    def _():
        pl.semaphore_wait(barrier, 12)

    def p_copy(a):
        return remote((tok, dlt)[a], XT.at[a, x, zq, yh], p_s.at[a], p_r.at[a], d_p)

    def p_recv(a):
        mine = XT.at[a, x, z, yh]
        return remote(mine, mine, p_s.at[a], p_r.at[a], d_p)

    def y_copy(a):
        mine = XT.at[a, x, z, yh]
        return remote(mine, mine, y_s.at[a], y_r.at[a], d_y)

    def y_recv(a):
        got = XT.at[a, x, z, 1 - yh]
        return remote(got, got, y_s.at[a], y_r.at[a], d_y)

    def z_copy(a, d):
        mine = XT.at[a, x, z]
        return remote(mine, mine, z_s.at[a, d], z_r.at[a, d], at(dp, rem(z + d, 8), yh, x))

    def z_recv(a, d):
        got = XT.at[a, x, rem(z + 8 - d, 8)]
        return remote(got, got, z_s.at[a, d], z_r.at[a, d], d_y)

    def x_copy(a, k, to_right):
        mine = XT.at[a, x, rem(z + 8 - k, 8)]
        if to_right:
            return remote(mine, mine, xr_s.at[a, k], xr_r.at[a, k], d_right)
        return remote(mine, mine, xl_s.at[a, k], xl_r.at[a, k], d_left)

    def x_recv(a, k, from_left):
        got = XT.at[a, left if from_left else right, rem(z + 8 - k, 8)]
        if from_left:
            return remote(got, got, xr_s.at[a, k], xr_r.at[a, k], d_right)
        return remote(got, got, xl_s.at[a, k], xl_r.at[a, k], d_left)

    def f_copy(a, k, to_right):
        got = XT.at[a, left if to_right else right, rem(z + 8 - k, 8)]
        return remote(got, got, f_s.at[a, k], f_r.at[a, k], d_right if to_right else d_left)

    def f_recv(a, k):
        got = XT.at[a, far, rem(z + 8 - k, 8)]
        return remote(got, got, f_s.at[a, k], f_r.at[a, k], d_right)

    def gather_p(a):
        @pl.when(at_home)
        def _():
            XT[a, x, z, yh] = (tok, dlt)[a][...]

        @pl.when(jnp.logical_not(at_home))
        def _():
            p_copy(a).start()

    def gather_y(a):
        @pl.when(jnp.logical_not(at_home))
        def _():
            p_recv(a).wait_recv()

        y_copy(a).start()

    def gather_z(a):
        y_recv(a).wait_recv()

        @pl.loop(1, 8)
        def _(d):
            z_copy(a, d).start()

    def forward(a, j):
        x_recv(a, 2 * j, True).wait_recv()
        f_copy(a, 2 * j, True).start()
        x_recv(a, 2 * j + 1, False).wait_recv()
        f_copy(a, 2 * j + 1, False).start()

    def gather_x(a, eager):
        @pl.loop(0, 4)
        def _(j):
            @pl.when(j > 0)
            def _():
                z_recv(a, 2 * j).wait_recv()

            x_copy(a, 2 * j, True).start()
            x_copy(a, 2 * j, False).start()
            z_recv(a, 2 * j + 1).wait_recv()
            x_copy(a, 2 * j + 1, True).start()
            x_copy(a, 2 * j + 1, False).start()
            if eager:
                @pl.when(j > 0)
                def _():
                    forward(a, j - 1)

    def gather_end(a):
        @pl.loop(0, 4)
        def _(j):
            x_recv(a, 2 * j, False).wait_recv()
            x_recv(a, 2 * j + 1, True).wait_recv()
            f_recv(a, 2 * j).wait_recv()
            f_recv(a, 2 * j + 1).wait_recv()

    def gather_drain(a):
        @pl.when(jnp.logical_not(at_home))
        def _():
            p_copy(a).wait_send()

        y_copy(a).wait_send()

        @pl.loop(1, 8)
        def _(d):
            z_copy(a, d).wait_send()

        @pl.loop(0, 4)
        def _(j):
            for k in (2 * j, 2 * j + 1):
                x_copy(a, k, True).wait_send()
                x_copy(a, k, False).wait_send()
            f_copy(a, 2 * j, True).wait_send()
            f_copy(a, 2 * j + 1, False).wait_send()

    def o_copy(a, p, to_right):
        return remote(
            PO.at[a, far, p], RXO.at[a, p], o_s.at[a, p], o_r.at[a, p], d_right if to_right else d_left
        )

    def w_copy(a, p, to_right):
        return remote(
            PO.at[a, right if to_right else left, p],
            RXR.at[a, p], w_s.at[a, p], w_r.at[a, p], d_right if to_right else d_left,
        )

    def c_copy(a, p, to_right):
        return remote(
            PO.at[a, right if to_right else left, p],
            RXC.at[a, p], c_s.at[a, p], c_r.at[a, p], d_right if to_right else d_left,
        )

    def zz_copy(a, p):
        return remote(PO.at[a, x, p], ZR.at[a, z], zz_s.at[a, p], zz_r.at[a, z], at(dp, p, yh, x))

    def zz_recv(a, s):
        return remote(ZR.at[a, s], ZR.at[a, s], zz_s.at[a, s], zz_r.at[a, s], d_y)

    def yy_copy(a):
        return remote(YS.at[a, 1 - yh], YR.at[a], yy_s.at[a], yy_r.at[a], d_y)

    def pp_copy(a):
        return remote(FS.at[a], FR.at[a], pp_s.at[a], pp_r.at[a], d_p)

    def sum_start(a):
        @pl.loop(0, 4)
        def _(q):
            o_copy(a, q, True).start()
            o_copy(a, q + 4, False).start()

        @pl.loop(0, 4)
        def _(q):
            w_copy(a, q + 4, True).start()
            w_copy(a, q, False).start()

    def sum_combine(a):
        @pl.loop(0, 4)
        def _(q):
            for p, to_right in ((q, True), (q + 4, False)):
                o_copy(a, p, to_right).wait_recv()
                to = right if to_right else left
                PO[a, to, p] = (PO[a, to, p].astype(F32) + RXO[a, p].astype(F32)).astype(BF16)
                c_copy(a, p, to_right).start()

    def sum_finish(a):
        @pl.loop(0, 4)
        def _(q):
            for p, to_right in ((q, True), (q + 4, False)):
                w_copy(a, p, to_right).wait_recv()
                c_copy(a, p, to_right).wait_recv()
                PO[a, x, p] = (
                    PO[a, x, p].astype(F32) + RXR[a, p].astype(F32) + RXC[a, p].astype(F32)
                ).astype(BF16)

                @pl.when(p != z)
                def _():
                    zz_copy(a, p).start()

    def sum_z(a):
        @pl.loop(1, 8)
        def _(d):
            zz_recv(a, rem(z + d, 8)).wait_recv()

        ZR[a, z] = PO[a, x, z]
        for half in range(2):
            total = ZR[a, 0, half].astype(F32)
            for s in range(1, 8):
                total = total + ZR[a, s, half].astype(F32)
            YS[a, half] = total.astype(BF16)
        yy_copy(a).start()

    def sum_y(a):
        yy_copy(a).wait_recv()
        FS[a] = (YS[a, yh].astype(F32) + YR[a].astype(F32)).astype(BF16)

        @pl.when(jnp.logical_not(at_home))
        def _():
            pp_copy(a).start()

    def sum_p(a):
        out = (bo, gi)[a]

        @pl.when(at_home)
        def _():
            out[...] = FS[a]

        @pl.when(jnp.logical_not(at_home))
        def _():
            pp_copy(a).wait_recv()
            out[...] = FR[a]

    def sum_drain(a):
        @pl.loop(0, 4)
        def _(q):
            for p, to_right in ((q, True), (q + 4, False)):
                o_copy(a, p, to_right).wait_send()
                w_copy(a, p, not to_right).wait_send()
                c_copy(a, p, to_right).wait_send()

        @pl.loop(1, 8)
        def _(d):
            zz_copy(a, rem(z + d, 8)).wait_send()

        yy_copy(a).wait_send()

        @pl.when(jnp.logical_not(at_home))
        def _():
            pp_copy(a).wait_send()

    def columns(a, tb):
        return jnp.concatenate(
            [XT[a, xx, 2 * tb + zb, yy] for zb in range(2) for yy in range(2) for xx in range(4)], axis=0
        )

    def scatter_rows(a, tb, total):
        rounded = total.astype(BF16)
        for zb in range(2):
            for yy in range(2):
                for xx in range(4):
                    jb = zb * 8 + yy * 4 + xx
                    PO[a, xx, 2 * tb + zb, yy] = rounded[jb * FB : (jb + 1) * FB]

    def dot(a, b):
        return jnp.dot(a, b, preferred_element_type=F32)

    def weights(w):
        loads[w].wait()
        WB[w] = MW[w].astype(BF16)

        @pl.loop(0, DS // 128)
        def _(n):
            cols = pl.ds(pl.multiple_of(n * 128, 128), 128)
            WT[w, cols, :] = MW[w, :, cols].T.astype(BF16)

    def core_copy(n, src, dst):
        return remote(src, dst, d_s.at[n], d_r.at[n], d_core)

    def chip_copy(n, src, dst):
        return remote(src, dst, e_s.at[n], e_r.at[n], d_chip)

    def grad(left_op, a):
        GR[...] = jnp.zeros((HID, DS), F32)

        @pl.loop(0, 4)
        def _(tb):
            GR[...] += lax.dot_general(
                left_op[tb], columns(a, tb), (((1,), (1,)), ((), ())), preferred_element_type=F32
            )

    def adamw(w, UO, out):
        loads[3 + w].wait()
        loads[6 + w].wait()

        @pl.loop(0, FFS // 8)
        def _(n):
            rows = pl.ds(pl.multiple_of(n * 8, 8), 8)
            gradient = GR[rows, :]
            moment = beta_first * MOM[w, rows, :] + (1.0 - beta_first) * gradient
            second = beta_second * SEC[w, rows, :] + (1.0 - beta_second) * gradient * gradient
            GR[rows, :] = (moment / correct_first) / (
                jnp.sqrt(second / correct_second) + adam_epsilon
            ) + weight_decay * MW[w, rows, :]

        UO[...] = GR[0:FFS, :].astype(BF16)
        store = pltpu.make_async_copy(UO, out, lsem.at[9 + w])
        store.start()
        return store

    gather_p(0)
    gather_p(1)
    weights(0)
    gather_y(0)
    gather_y(1)
    gather_z(0)
    weights(1)
    gather_x(0, True)
    gather_z(1)
    forward(0, 3)
    weights(2)
    gather_end(0)
    gather_x(1, False)

    @pl.loop(0, 2)
    def _(k):
        cols = columns(0, 2 * (1 - core) + k)
        SD[k, 0] = dot(WB[0], cols)[:PAD].astype(BF16)
        SD[k, 1] = dot(WB[1], cols)[:PAD].astype(BF16)

    core_copy(0, SD, RD).start()

    @pl.loop(0, 2)
    def _(k):
        cols = columns(0, 2 * core + k)
        GUO[k, 0] = dot(WB[0], cols)[:PAD]
        GUO[k, 1] = dot(WB[1], cols)[:PAD]

    core_copy(0, SD, RD).wait_recv()

    @pl.loop(0, 2)
    def _(k):
        GUO[k] = GUO[k] + RD[k].astype(F32)
        SY[k] = GUO[k].astype(BF16)
        chip_copy(k, SY.at[k], RY.at[k]).start()

    @pl.loop(0, 4)
    def _(j):
        forward(1, j)

    @pl.loop(0, 2)
    def _(k):
        chip_copy(k, SY.at[k], RY.at[k]).wait_recv()
        gate_in = GUO[k, 0] + RY[k, 0].astype(F32)
        up_in = GUO[k, 1] + RY[k, 1].astype(F32)
        sig = jax.nn.sigmoid(gate_in)
        active = gate_in * sig
        ACT[k] = active
        US[k] = up_in * (sig * (1.0 + gate_in * (1.0 - sig)))
        mine = HD.at[2 * core + k]
        HD[2 * core + k, 0:PAD, :] = (active * up_in).astype(BF16)
        core_copy(1 + k, mine, mine).start()

    @pl.loop(0, 2)
    def _(k):
        theirs = HD.at[2 * (1 - core) + k]
        core_copy(1 + k, theirs, theirs).wait_recv()

    @pl.loop(0, 4)
    def _(tb):
        scatter_rows(0, tb, dot(WT[2], HD[tb]))

    sum_start(0)
    gather_end(1)

    @pl.loop(0, 2)
    def _(k):
        SD2[k] = dot(WB[2], columns(1, 2 * (1 - core) + k))[:PAD].astype(BF16)

    core_copy(3, SD2, RD2).start()

    @pl.loop(0, 2)
    def _(k):
        DHO[k] = dot(WB[2], columns(1, 2 * core + k))[:PAD]

    core_copy(3, SD2, RD2).wait_recv()

    @pl.loop(0, 2)
    def _(k):
        DHO[k] = DHO[k] + RD2[k].astype(F32)
        SY2[k] = DHO[k].astype(BF16)
        chip_copy(2 + k, SY2.at[k], RY2.at[k]).start()

    sum_combine(0)

    @pl.loop(0, 2)
    def _(k):
        chip_copy(2 + k, SY2.at[k], RY2.at[k]).wait_recv()
        d_hidden = DHO[k] + RY2[k].astype(F32)
        gate, up = DG.at[2 * core + k], DU.at[2 * core + k]
        DG[2 * core + k, 0:PAD, :] = (d_hidden * US[k]).astype(BF16)
        DU[2 * core + k, 0:PAD, :] = (d_hidden * ACT[k]).astype(BF16)
        core_copy(4 + k, gate, gate).start()
        core_copy(6 + k, up, up).start()

    @pl.loop(0, 2)
    def _(k):
        gate, up = DG.at[2 * (1 - core) + k], DU.at[2 * (1 - core) + k]
        core_copy(4 + k, gate, gate).wait_recv()
        core_copy(6 + k, up, up).wait_recv()

    @pl.loop(0, 4)
    def _(tb):
        scatter_rows(1, tb, dot(WT[0], DG[tb]) + dot(WT[1], DU[tb]))

    sum_start(1)
    sum_finish(0)
    grad(HD, 1)
    store_down = adamw(2, UO2, ud)
    sum_combine(1)
    sum_z(0)
    grad(DG, 0)
    store_gate = adamw(0, UO0, ug)
    sum_y(0)
    grad(DU, 0)
    store_up = adamw(1, UO1, uu)
    sum_finish(1)
    sum_p(0)
    sum_z(1)
    gather_drain(0)
    gather_drain(1)
    sum_drain(0)
    core_copy(0, SD, RD).wait_send()
    core_copy(3, SD2, RD2).wait_send()

    @pl.loop(0, 2)
    def _(k):
        hid, gate, up = HD.at[2 * core + k], DG.at[2 * core + k], DU.at[2 * core + k]
        chip_copy(k, SY.at[k], RY.at[k]).wait_send()
        chip_copy(2 + k, SY2.at[k], RY2.at[k]).wait_send()
        core_copy(1 + k, hid, hid).wait_send()
        core_copy(4 + k, gate, gate).wait_send()
        core_copy(6 + k, up, up).wait_send()

    sum_y(1)
    sum_p(1)
    sum_drain(1)
    store_down.wait()
    store_gate.wait()
    store_up.wait()


def step(tok, dlt, states):
    def vmem(*shape, dtype=BF16):
        return pltpu.VMEM(shape, dtype)

    dma = pltpu.SemaphoreType.DMA
    out = jax.ShapeDtypeStruct
    shard, update = out((FB, TB), BF16), out((FFS, DS), BF16)
    in_vmem = pl.BlockSpec(memory_space=pltpu.VMEM)
    in_any = pl.BlockSpec(memory_space=pl.ANY)
    scratch = [
        vmem(2, 4, 8, 2, FB, TB),
        vmem(2, 4, 8, 2, FB, TB),
        vmem(2, 8, 2, FB, TB),
        vmem(2, 8, 2, FB, TB),
        vmem(2, 8, 2, FB, TB),
        vmem(2, 8, 2, FB, TB),
        vmem(2, 2, FB, TB),
        vmem(2, FB, TB),
        vmem(2, FB, TB),
        vmem(2, FB, TB),
        vmem(3, HID, DS, dtype=F32),
        vmem(3, FFS, DS, dtype=F32),
        vmem(3, FFS, DS, dtype=F32),
        vmem(3, HID, DS),
        vmem(3, DS, HID),
        vmem(4, HID, TB),
        vmem(4, HID, TB),
        vmem(4, HID, TB),
        vmem(2, 2, PAD, TB, dtype=F32),
        vmem(2, PAD, TB, dtype=F32),
        vmem(2, PAD, TB, dtype=F32),
        vmem(2, PAD, TB, dtype=F32),
        vmem(2, 2, PAD, TB),
        vmem(2, 2, PAD, TB),
        vmem(2, 2, PAD, TB),
        vmem(2, 2, PAD, TB),
        vmem(2, PAD, TB),
        vmem(2, PAD, TB),
        vmem(2, PAD, TB),
        vmem(2, PAD, TB),
        vmem(HID, DS, dtype=F32),
        vmem(FFS, DS),
        vmem(FFS, DS),
        vmem(FFS, DS),
        dma((12,)),
        dma((2,)), dma((2,)),
        dma((2,)), dma((2,)),
        dma((2, 8)), dma((2, 8)),
        dma((2, 8)), dma((2, 8)),
        dma((2, 8)), dma((2, 8)),
        dma((2, 8)), dma((2, 8)),
        dma((2, 8)), dma((2, 8)),
        dma((2, 8)), dma((2, 8)),
        dma((2, 8)), dma((2, 8)),
        dma((2, 8)), dma((2, 8)),
        dma((2,)), dma((2,)),
        dma((2,)), dma((2,)),
        dma((8,)), dma((8,)),
        dma((4,)), dma((4,)),
    ]
    return pl.pallas_call(
        kernel,
        out_shape=[shard, shard, update, update, update],
        in_specs=[in_vmem] * 2 + [in_any] * 9,
        out_specs=[in_vmem] * 2 + [in_any] * 3,
        scratch_shapes=scratch,
        compiler_params=pltpu.CompilerParams(
            collective_id=0, has_side_effects=True, vmem_limit_bytes=58 * 1024 * 1024
        ),
        cost_estimate=pl.CostEstimate(flops=5_100_000_000, bytes_accessed=12_000_000, transcendentals=1_000_000),
        name="fused_step",
    )(tok, dlt, *states)


def body(tokens, cotangent, pass_counts, group_ids, token_rollout, *states):
    reward = pass_counts.astype(F32) / TESTS
    same_group = (group_ids[:, None] == group_ids[None, :]).astype(F32)
    baseline = jnp.sum(same_group * reward[None, :], axis=1) / jnp.sum(same_group, axis=1)
    advantage = reward - baseline
    picker = (token_rollout[:, None] == jnp.arange(ROLL, dtype=jnp.int32)[None, :]).astype(F32)
    token_adv = jnp.sum(picker * advantage[None, :], axis=1)
    delta = (-token_adv[:, None] * cotangent.astype(F32)).astype(BF16)
    block_out, grad_input, update_gate, update_up, update_down = step(tokens.T, delta.T, states)
    return block_out.T, grad_input.T, update_gate, update_up, update_down


def solution(mesh):
    act, rep, weight = P("dp", "fsdp"), P(), P("fsdp", "dp")
    return jax.shard_map(
        body,
        mesh=mesh,
        in_specs=(act, act, rep, rep, P("dp")) + (weight,) * 9,
        out_specs=(act, act, weight, weight, weight),
        check_vma=False,
    )
```

time: 1280 us -> 155 us (0.12)
  the two profiles are of different devices: /device:TPU:8 before, /device:TPU:1 now
where the time goes in v1:
time: 155 us; the launch traced here: 154 us
  Pallas kernels  143 us (92%)
  local copies, waits for them, and re-layouts  6.42 us (4%)
  other arithmetic  4.42 us (3%)
    pallas_call x1, Pallas kernels, step(): pl.pallas_call(kernel, out_shape=[shard, shard, update, update, update],...  143 us
    unnamed x9, local copies, waits for them, and re-layouts  6.42 us

profile of v1, /device:TPU:1, one launch (start us, length us, event | category | flops | bytes accessed | tf_op | source)
XLA Modules:
  0.0 154.2 jit_solution(12159798662083018219)
XLA Ops:
  0.6 0.7 convert_multiply_fusion
  1.3 0.9 fusion.2
  2.2 0.7 divide_subtract_fusion
  2.9 0.8 select_reduce_fusion
  3.7 1.4 fusion.dlt
  5.1 142.7 %fused_step.1 = (bf16[80,256]{1,0:T(8,128)(2,1)}, bf16[80,256]{1,0:T(8,128)(2,1)}, bf16[216,1280]{1,0:T(8,128)(2,1)}, bf16[216,1280]{1,0:T(8,128)(2,1)}, bf16[216,1280]{1,0:T(8,128)(2,1)}) custom-call(bf16[80,256]{1,0:T(8,128)(2,1)} %bitcast.7, bf16[80,256]{1,0:T(8,128)(2,1)} %fusion.dlt, f32[216,1280]{1,0:T(8,128)} %mg.1, f32[216,1280]{1,0:T(8,128)} %mu.1, ...), custom_call_target="tpu_custom_call" | custom-call | flops 5100000256 | bytes 12000000 | tf_op jit(solution)/shard_map/fused_step/pallas_call | solution.py:598
  147.8 0.0 copy-start.1
  147.8 1.5 copy.24
  149.3 1.4 copy.25
  150.7 0.0 copy-start
  150.7 1.9 %copy.26 = bf16[216,1280]{1,0:T(8,128)(2,1)} copy(bf16[216,1280]{1,0:T(8,128)(2,1)} %get-tuple-element.24) | data formatting | bytes 1105920
  152.6 0.0 copy-done.1
  152.6 0.8 copy.27
  153.4 0.0 copy-done
  153.4 0.8 copy.28
  (1 shorter events, 0.0 us)
Async XLA Ops:
  147.8 4.8 %copy-start.1 = (bf16[216,1280]{1,0:T(8,128)(2,1)S(1)}, bf16[216,1280]{1,0:T(8,128)(2,1)}, u32[]{:S(2)}) copy-start(bf16[216,1280]{1,0:T(8,128)(2,1)} %get-tuple-element.25) | copy-start | bytes 1658884
  150.7 2.8 %copy-start = (bf16[216,1280]{1,0:T(8,128)(2,1)S(1)}, bf16[216,1280]{1,0:T(8,128)(2,1)}, u32[]{:S(2)}) copy-start(bf16[216,1280]{1,0:T(8,128)(2,1)} %get-tuple-element.26) | copy-start | bytes 1658884

commit v2 on v1

v2 whole, which is shorter than its diff:
```python
import jax
import jax.numpy as jnp
from jax import lax
from jax.experimental import pallas as pl
from jax.experimental.pallas import tpu as pltpu
from jax.sharding import PartitionSpec as P

ROLL = 64
TESTS = 8
beta_first = 0.9
beta_second = 0.95
adam_epsilon = 1e-08
weight_decay = 0.1
correct_first = 1.0 - 0.9**10
correct_second = 1.0 - 0.95**10

FFS = 216
PAD = 224
HID = 256
DS = 1280
FB = 80
TB = 256
F32 = jnp.float32
BF16 = jnp.bfloat16


def rem(a, b):
    return lax.rem(a, jnp.int32(b))


def div(a, b):
    return lax.div(a, jnp.int32(b))


def remote(src, dst, send, recv, device):
    return pltpu.make_async_remote_copy(
        src_ref=src,
        dst_ref=dst,
        send_sem=send,
        recv_sem=recv,
        device_id=device,
        device_id_type=pl.DeviceIdType.MESH,
    )


def kernel(
    tok, cot, counts, groups, rolls, mg, mu, md, og, ou, od, sg, su, sd,
    bo, gi, ug, uu, ud,
    TT, XT, PO, RV, RXO, RXR, RXC, ZR, YS, FR,
    MW, MOM, SEC, WB, WT, HD, DG, DU, GUO, ACT, US, DHO,
    SD, RD, SY, RY, SD2, RD2, SY2, RY2, GR, UO0, UO1, UO2,
    lsem, z_s, z_r, xr_s, xr_r, xl_s, xl_r, f_s, f_r,
    v_s, v_r, u_s, u_r, o_s, o_r, w_s, w_r, c_s, c_r, zz_s, zz_r, q_s, q_r,
    d_s, d_r, e_s, e_r,
):
    dp = lax.axis_index("dp")
    fs = lax.axis_index("fsdp")
    z, yh, x = div(fs, 8), rem(div(fs, 4), 2), rem(fs, 4)
    core = rem(dp, 2)
    right, left, far = rem(x + 1, 4), rem(x + 3, 4), rem(x + 2, 4)

    def at(dp_, z_, y_, x_):
        return (dp_, z_ * 8 + y_ * 4 + x_)

    d_right, d_left = at(dp, z, yh, right), at(dp, z, yh, left)
    home = div(z, 2)
    own = 2 * dp + rem(z, 2)
    at_home = home == dp
    d_y = at(dp, z, 1 - yh, x)
    d_core = at(dp + 1 - 2 * core, z, yh, x)
    d_chip = at(rem(dp + 2, 4), z, yh, x)

    srcs = (mg, mu, md, og, ou, od, sg, su, sd)
    loads = []
    for n, src in enumerate(srcs):
        dst = (MW, MOM, SEC)[n // 3].at[n % 3, pl.ds(0, FFS)]
        loads.append(pltpu.make_async_copy(src, dst, lsem.at[n]))
    for load in loads:
        load.start()

    for w in range(3):
        MW[w, FFS:HID, :] = jnp.zeros((HID - FFS, DS), F32)
    for buf in (HD, DG, DU):
        for n in range(4):
            buf[n, PAD:HID, :] = jnp.zeros((HID - PAD, TB), BF16)

    def is_self(n, t):
        return jnp.logical_and(jnp.logical_and(at_home, n == 0), t == yh)

    barrier = pltpu.get_barrier_semaphore()

    def greet(peer):
        pl.semaphore_signal(barrier, inc=1, device_id=peer, device_id_type=pl.DeviceIdType.MESH)

    for peer in (d_right, d_left, d_core, d_chip, d_y):
        greet(peer)

    @pl.loop(1, 8)
    def _(n):
        greet(at(dp, rem(z + n, 8), yh, x))

    @pl.loop(0, 8)
    def _(n):
        for t in range(2):
            @pl.when(jnp.logical_not(is_self(n, t)))
            def _():
                greet(at(div(rem(z + n, 8), 2), 2 * dp + rem(z + n, 2), t, x))

    reward = counts[...].astype(F32) / TESTS
    group = groups[...].astype(F32)
    group_col = jnp.broadcast_to(group, (ROLL, ROLL)).T
    same = (group_col == group).astype(F32)
    baseline = jnp.sum(same * reward, axis=1, keepdims=True) / jnp.sum(same, axis=1, keepdims=True)
    reward_col = jnp.broadcast_to(reward, (ROLL, ROLL)).T[:, 0:1]
    advantage = reward_col - baseline
    rollout = lax.broadcasted_iota(jnp.int32, (ROLL, TB), 0)
    token_adv = jnp.sum(jnp.where(rollout == rolls[...], advantage, 0.0), axis=0, keepdims=True)
    TT[0] = tok[...]
    TT[1] = (-token_adv * cot[...].astype(F32)).astype(BF16)

    @pl.when(at_home)
    def _():
        pl.semaphore_wait(barrier, 27)

    @pl.when(jnp.logical_not(at_home))
    def _():
        pl.semaphore_wait(barrier, 28)

    def z_copy(a, n, t):
        return remote(
            TT.at[a], XT.at[a, x, own, yh], z_s.at[a, n, t], z_r.at[a, n, yh], at(home, rem(own + n, 8), t, x)
        )

    def z_start(a, n):
        for t in range(2):
            @pl.when(jnp.logical_and(jnp.logical_not(is_self(n, t)), jnp.logical_or(n >= 2, t == yh)))
            def _():
                z_copy(a, n, t).start()

    def z_recv(a, k):
        for s in range(2):
            @pl.when(jnp.logical_and(jnp.logical_not(is_self(k, s)), jnp.logical_or(k >= 2, s == yh)))
            def _():
                got = XT.at[a, x, rem(z + 8 - k, 8), s]
                remote(got, got, z_s.at[a, k, s], z_r.at[a, k, s], d_right).wait_recv()

    def piece(a, xx, k):
        block = XT.at[a, xx, rem(z + 8 - k, 8)]
        return block.at[yh] if isinstance(k, int) and k < 2 else block

    def x_copy(a, k, to_right):
        mine = piece(a, x, k)
        if to_right:
            return remote(mine, mine, xr_s.at[a, k], xr_r.at[a, k], d_right)
        return remote(mine, mine, xl_s.at[a, k], xl_r.at[a, k], d_left)

    def x_recv(a, k, from_left):
        got = piece(a, left if from_left else right, k)
        if from_left:
            return remote(got, got, xr_s.at[a, k], xr_r.at[a, k], d_right)
        return remote(got, got, xl_s.at[a, k], xl_r.at[a, k], d_left)

    def f_copy(a, k, to_right):
        got = piece(a, left if to_right else right, k)
        return remote(got, got, f_s.at[a, k], f_r.at[a, k], d_right if to_right else d_left)

    def f_recv(a, k):
        got = piece(a, far, k)
        return remote(got, got, f_s.at[a, k], f_r.at[a, k], d_right)

    def v_copy(a, k, xx):
        mine = XT.at[a, xx, rem(z + 8 - k, 8), yh]
        return remote(mine, mine, v_s.at[a, k, xx], v_r.at[a, k, xx], d_y)

    def v_recv(a, k, xx):
        got = XT.at[a, xx, rem(z + 8 - k, 8), 1 - yh]
        return remote(got, got, v_s.at[a, k, xx], v_r.at[a, k, xx], d_y)

    def gather_home(a):
        @pl.when(at_home)
        def _():
            XT[a, x, own, yh] = TT[a]

    def forward(a, j):
        x_recv(a, 2 * j, True).wait_recv()
        f_copy(a, 2 * j, True).start()
        x_recv(a, 2 * j + 1, False).wait_recv()
        f_copy(a, 2 * j + 1, False).start()

    def forward_first(a):
        forward(a, 0)
        x_recv(a, 0, False).wait_recv()
        x_recv(a, 1, True).wait_recv()

    def v_start(a, *sides):
        for k in range(2):
            for n in sides:
                v_copy(a, k, n).start()

    def forward_far(a):
        for k in range(2):
            f_recv(a, k).wait_recv()

    def gather_step(a, j):
        for k in (2 * j, 2 * j + 1):
            z_recv(a, k)
            x_copy(a, k, True).start()
            x_copy(a, k, False).start()
            if a == 0:
                @pl.when(k < 5)
                def _():
                    z_start(0, k + 3)

                @pl.when(k >= 5)
                def _():
                    z_start(1, k - 5)

    def gather_x(a):
        gather_step(a, 0)
        if a == 0:
            v_start(0, x)
            gather_step(a, 1)
            forward_first(a)
            v_start(0, left, right)

            @pl.loop(2, 4)
            def _(j):
                gather_step(a, j)
                forward(a, j - 1)

            @pl.loop(3, 8)
            def _(n):
                z_start(1, n)
        else:
            @pl.loop(1, 4)
            def _(j):
                gather_step(a, j)

    def gather_end(a):
        @pl.loop(1, 4)
        def _(j):
            x_recv(a, 2 * j, False).wait_recv()
            x_recv(a, 2 * j + 1, True).wait_recv()
            f_recv(a, 2 * j).wait_recv()
            f_recv(a, 2 * j + 1).wait_recv()

        for k in range(2):
            @pl.loop(0, 4)
            def _(n):
                v_recv(a, k, n).wait_recv()

    def gather_drain(a):
        for k in range(8):
            for t in range(2):
                @pl.when(jnp.logical_and(jnp.logical_not(is_self(k, t)), jnp.logical_or(k >= 2, t == yh)))
                def _():
                    z_copy(a, k, t).wait_send()
            x_copy(a, k, True).wait_send()
            x_copy(a, k, False).wait_send()
            f_copy(a, k, k % 2 == 0).wait_send()
        for k in range(2):
            @pl.loop(0, 4)
            def _(n):
                v_copy(a, k, n).wait_send()

    def place(k):
        return rem(z + k, 8)

    def late(k):
        return isinstance(k, int) and k >= 6

    def part(a, xx, k):
        block = PO.at[a, xx, place(k)]
        return block.at[yh] if late(k) else block

    def slot(buf, a, k):
        return buf.at[a, k, 0] if late(k) else buf.at[a, k]

    def u_copy(a, k, n):
        return remote(
            PO.at[a, n, place(k), 1 - yh], RV.at[a, k - 6, n], u_s.at[a, k - 6, n], u_r.at[a, k - 6, n], d_y
        )

    def o_copy(a, k, to_right):
        return remote(
            part(a, far, k), slot(RXO, a, k), o_s.at[a, k], o_r.at[a, k], d_right if to_right else d_left
        )

    def w_copy(a, k, to_right):
        return remote(
            part(a, right if to_right else left, k),
            slot(RXR, a, k), w_s.at[a, k], w_r.at[a, k], d_right if to_right else d_left,
        )

    def c_copy(a, k, to_right):
        return remote(
            part(a, right if to_right else left, k),
            slot(RXC, a, k), c_s.at[a, k], c_r.at[a, k], d_right if to_right else d_left,
        )

    def zz_copy(a, k):
        dst = ZR.at[a, k, yh] if late(k) else ZR.at[a, k]
        return remote(part(a, x, k), dst, zz_s.at[a, k], zz_r.at[a, k], at(dp, place(k), yh, x))

    def q_copy(a, s):
        return remote(YS.at[a, s], FR.at[a, yh], q_s.at[a, s], q_r.at[a, yh], at(home, own, s, x))

    def halves(j):
        return ((2 * j, True), (2 * j + 1, False))

    def o_start(a, j):
        for k, to_right in halves(j):
            o_copy(a, k, to_right).start()

    def w_start(a, j):
        for k, to_right in halves(j):
            w_copy(a, k, not to_right).start()

    def sum_start(a):
        for k in (6, 7):
            @pl.loop(0, 4)
            def _(n):
                u_copy(a, k, n).start()

        o_start(a, 0)
        o_start(a, 1)
        w_start(a, 0)
        if a == 0:
            o_start(a, 2)
            w_start(a, 1)
            w_start(a, 2)

    def fold_y(a):
        for k in (6, 7):
            @pl.loop(0, 4)
            def _(n):
                u_copy(a, k, n).wait_recv()
                mine = PO.at[a, n, place(k), yh]
                mine[...] = (mine[...].astype(F32) + RV[a, k - 6, n].astype(F32)).astype(BF16)

    def combine(a, j):
        for k, to_right in halves(j):
            o_copy(a, k, to_right).wait_recv()
            mine, got = part(a, right if to_right else left, k), slot(RXO, a, k)
            mine[...] = (mine[...].astype(F32) + got[...].astype(F32)).astype(BF16)
            c_copy(a, k, to_right).start()

    def finish(a, j):
        for k, to_right in halves(j):
            w_copy(a, k, not to_right).wait_recv()
            c_copy(a, k, to_right).wait_recv()
            mine = part(a, x, k)
            mine[...] = (
                mine[...].astype(F32) + slot(RXR, a, k)[...].astype(F32) + slot(RXC, a, k)[...].astype(F32)
            ).astype(BF16)
            if late(k):
                zz_copy(a, k).start()
            else:
                @pl.when(k > 0)
                def _():
                    zz_copy(a, k).start()

    def sum_finish(a):
        @pl.loop(0, 3)
        def _(j):
            finish(a, j)

        finish(a, 3)

    def sum_z(a):
        for k in range(1, 8):
            zz_copy(a, k).wait_recv()
        for s in range(2):
            total = PO[a, x, z, s].astype(F32)
            for k in range(1, 6):
                total = total + ZR[a, k, s].astype(F32)

            @pl.when(s == yh)
            def _():
                YS[a, s] = (total + ZR[a, 6, s].astype(F32) + ZR[a, 7, s].astype(F32)).astype(BF16)

            @pl.when(s != yh)
            def _():
                YS[a, s] = total.astype(BF16)

            @pl.when(jnp.logical_not(is_self(0, s)))
            def _():
                q_copy(a, s).start()

    def sum_end(a):
        for s in range(2):
            @pl.when(is_self(0, s))
            def _():
                FR[a, s] = YS[a, s]

            @pl.when(jnp.logical_not(is_self(0, s)))
            def _():
                remote(FR.at[a, s], FR.at[a, s], q_s.at[a, s], q_r.at[a, s], d_right).wait_recv()

        (bo, gi)[a][...] = (FR[a, 0].astype(F32) + FR[a, 1].astype(F32)).astype(BF16)

    def sum_drain(a):
        for k in (6, 7):
            @pl.loop(0, 4)
            def _(n):
                u_copy(a, k, n).wait_send()

        for j in range(4):
            for k, to_right in halves(j):
                o_copy(a, k, to_right).wait_send()
                w_copy(a, k, not to_right).wait_send()
                c_copy(a, k, to_right).wait_send()
                if k > 0:
                    zz_copy(a, k).wait_send()

        for s in range(2):
            @pl.when(jnp.logical_not(is_self(0, s)))
            def _():
                q_copy(a, s).wait_send()

    def columns(a, tb):
        return jnp.concatenate(
            [XT[a, xx, 2 * tb + zb, yy] for zb in range(2) for yy in range(2) for xx in range(4)], axis=0
        )

    def scatter_rows(a, tb, total):
        rounded = total.astype(BF16)
        for zb in range(2):
            for yy in range(2):
                for xx in range(4):
                    jb = zb * 8 + yy * 4 + xx
                    PO[a, xx, 2 * tb + zb, yy] = rounded[jb * FB : (jb + 1) * FB]

    def dot(a, b):
        return jnp.dot(a, b, preferred_element_type=F32)

    def weights(w):
        loads[w].wait()
        WB[w] = MW[w].astype(BF16)

        @pl.loop(0, DS // 128)
        def _(n):
            cols = pl.ds(pl.multiple_of(n * 128, 128), 128)
            WT[w, cols, :] = MW[w, :, cols].T.astype(BF16)

    def core_copy(n, src, dst):
        return remote(src, dst, d_s.at[n], d_r.at[n], d_core)

    def chip_copy(n, src, dst):
        return remote(src, dst, e_s.at[n], e_r.at[n], d_chip)

    def grad(left_op, a):
        GR[...] = jnp.zeros((HID, DS), F32)

        @pl.loop(0, 4)
        def _(tb):
            GR[...] += lax.dot_general(
                left_op[tb], columns(a, tb), (((1,), (1,)), ((), ())), preferred_element_type=F32
            )

    def adamw(w, UO, out):
        loads[3 + w].wait()
        loads[6 + w].wait()

        @pl.loop(0, FFS // 8)
        def _(n):
            rows = pl.ds(pl.multiple_of(n * 8, 8), 8)
            gradient = GR[rows, :]
            moment = beta_first * MOM[w, rows, :] + (1.0 - beta_first) * gradient
            second = beta_second * SEC[w, rows, :] + (1.0 - beta_second) * gradient * gradient
            GR[rows, :] = (moment / correct_first) / (
                jnp.sqrt(second / correct_second) + adam_epsilon
            ) + weight_decay * MW[w, rows, :]

        UO[...] = GR[0:FFS, :].astype(BF16)
        store = pltpu.make_async_copy(UO, out, lsem.at[9 + w])
        store.start()
        return store

    gather_home(0)

    @pl.loop(0, 3)
    def _(n):
        z_start(0, n)

    gather_home(1)
    weights(0)
    weights(1)
    gather_x(0)
    forward_far(0)
    v_start(0, far)
    forward(0, 3)
    weights(2)
    gather_x(1)
    gather_end(0)

    @pl.loop(0, 2)
    def _(k):
        cols = columns(0, 2 * (1 - core) + k)
        SD[k, 0] = dot(WB[0], cols)[:PAD].astype(BF16)
        SD[k, 1] = dot(WB[1], cols)[:PAD].astype(BF16)
        core_copy(8 * k, SD.at[k], RD.at[k]).start()

    @pl.loop(0, 2)
    def _(k):
        cols = columns(0, 2 * core + k)
        core_copy(8 * k, SD.at[k], RD.at[k]).wait_recv()
        gate = dot(WB[0], cols)[:PAD] + RD[k, 0].astype(F32)
        up = dot(WB[1], cols)[:PAD] + RD[k, 1].astype(F32)
        GUO[k, 0] = gate
        GUO[k, 1] = up
        SY[k, 0] = gate.astype(BF16)
        SY[k, 1] = up.astype(BF16)
        chip_copy(k, SY.at[k], RY.at[k]).start()

    forward_first(1)

    @pl.loop(1, 4)
    def _(j):
        forward(1, j)

    @pl.loop(0, 2)
    def _(k):
        chip_copy(k, SY.at[k], RY.at[k]).wait_recv()
        gate_in = GUO[k, 0] + RY[k, 0].astype(F32)
        up_in = GUO[k, 1] + RY[k, 1].astype(F32)
        sig = jax.nn.sigmoid(gate_in)
        active = gate_in * sig
        ACT[k] = active
        US[k] = up_in * (sig * (1.0 + gate_in * (1.0 - sig)))
        mine = HD.at[2 * core + k]
        HD[2 * core + k, 0:PAD, :] = (active * up_in).astype(BF16)
        core_copy(1 + k, mine, mine).start()

    forward_far(1)
    v_start(1, x, left, right, far)

    @pl.loop(0, 2)
    def _(k):
        theirs = HD.at[2 * (1 - core) + k]
        core_copy(1 + k, theirs, theirs).wait_recv()

    @pl.loop(0, 4)
    def _(tb):
        scatter_rows(0, tb, dot(WT[2], HD[tb]))

    sum_start(0)
    gather_end(1)

    @pl.loop(0, 2)
    def _(k):
        SD2[k] = dot(WB[2], columns(1, 2 * (1 - core) + k))[:PAD].astype(BF16)

    core_copy(3, SD2, RD2).start()

    @pl.loop(0, 2)
    def _(k):
        DHO[k] = dot(WB[2], columns(1, 2 * core + k))[:PAD]

    core_copy(3, SD2, RD2).wait_recv()

    @pl.loop(0, 2)
    def _(k):
        DHO[k] = DHO[k] + RD2[k].astype(F32)
        SY2[k] = DHO[k].astype(BF16)
        chip_copy(2 + k, SY2.at[k], RY2.at[k]).start()

    combine(0, 0)
    fold_y(0)
    o_start(0, 3)
    w_start(0, 3)
    for j in range(1, 4):
        combine(0, j)
    grad(HD, 1)
    store_down = adamw(2, UO2, ud)

    @pl.loop(0, 2)
    def _(k):
        chip_copy(2 + k, SY2.at[k], RY2.at[k]).wait_recv()
        d_hidden = DHO[k] + RY2[k].astype(F32)
        gate, up = DG.at[2 * core + k], DU.at[2 * core + k]
        DG[2 * core + k, 0:PAD, :] = (d_hidden * US[k]).astype(BF16)
        DU[2 * core + k, 0:PAD, :] = (d_hidden * ACT[k]).astype(BF16)
        core_copy(4 + k, gate, gate).start()
        core_copy(6 + k, up, up).start()

    @pl.loop(0, 2)
    def _(k):
        gate, up = DG.at[2 * (1 - core) + k], DU.at[2 * (1 - core) + k]
        core_copy(4 + k, gate, gate).wait_recv()
        core_copy(6 + k, up, up).wait_recv()

    @pl.loop(0, 4)
    def _(tb):
        scatter_rows(1, tb, dot(WT[0], DG[tb]) + dot(WT[1], DU[tb]))

    sum_start(1)
    sum_finish(0)
    combine(1, 0)
    o_start(1, 2)
    w_start(1, 1)
    grad(DG, 0)
    store_gate = adamw(0, UO0, ug)
    fold_y(1)
    combine(1, 1)
    o_start(1, 3)
    w_start(1, 2)
    finish(1, 0)
    sum_z(0)
    combine(1, 2)
    w_start(1, 3)
    finish(1, 1)
    grad(DU, 0)
    store_up = adamw(1, UO1, uu)
    combine(1, 3)
    finish(1, 2)
    finish(1, 3)
    sum_end(0)
    sum_z(1)
    gather_drain(0)
    gather_drain(1)
    sum_drain(0)
    for k in range(2):
        core_copy(8 * k, SD.at[k], RD.at[k]).wait_send()
    core_copy(3, SD2, RD2).wait_send()

    @pl.loop(0, 2)
    def _(k):
        hid, gate, up = HD.at[2 * core + k], DG.at[2 * core + k], DU.at[2 * core + k]
        chip_copy(k, SY.at[k], RY.at[k]).wait_send()
        chip_copy(2 + k, SY2.at[k], RY2.at[k]).wait_send()
        core_copy(1 + k, hid, hid).wait_send()
        core_copy(4 + k, gate, gate).wait_send()
        core_copy(6 + k, up, up).wait_send()

    sum_end(1)
    sum_drain(1)
    store_down.wait()
    store_gate.wait()
    store_up.wait()


def step(*inputs):
    def vmem(*shape, dtype=BF16):
        return pltpu.VMEM(shape, dtype)

    dma = pltpu.SemaphoreType.DMA
    out = jax.ShapeDtypeStruct
    shard, update = out((FB, TB), BF16), out((FFS, DS), BF16)
    in_vmem = pl.BlockSpec(memory_space=pltpu.VMEM)
    in_any = pl.BlockSpec(memory_space=pl.ANY)
    scratch = [
        vmem(2, FB, TB),
        vmem(2, 4, 8, 2, FB, TB),
        vmem(2, 4, 8, 2, FB, TB),
        vmem(2, 2, 4, FB, TB),
        vmem(2, 8, 2, FB, TB),
        vmem(2, 8, 2, FB, TB),
        vmem(2, 8, 2, FB, TB),
        vmem(2, 8, 2, FB, TB),
        vmem(2, 2, FB, TB),
        vmem(2, 2, FB, TB),
        vmem(3, HID, DS, dtype=F32),
        vmem(3, FFS, DS, dtype=F32),
        vmem(3, FFS, DS, dtype=F32),
        vmem(3, HID, DS),
        vmem(3, DS, HID),
        vmem(4, HID, TB),
        vmem(4, HID, TB),
        vmem(4, HID, TB),
        vmem(2, 2, PAD, TB, dtype=F32),
        vmem(2, PAD, TB, dtype=F32),
        vmem(2, PAD, TB, dtype=F32),
        vmem(2, PAD, TB, dtype=F32),
        vmem(2, 2, PAD, TB),
        vmem(2, 2, PAD, TB),
        vmem(2, 2, PAD, TB),
        vmem(2, 2, PAD, TB),
        vmem(2, PAD, TB),
        vmem(2, PAD, TB),
        vmem(2, PAD, TB),
        vmem(2, PAD, TB),
        vmem(HID, DS, dtype=F32),
        vmem(FFS, DS),
        vmem(FFS, DS),
        vmem(FFS, DS),
        dma((12,)),
        dma((2, 8, 2)), dma((2, 8, 2)),
        dma((2, 8)), dma((2, 8)),
        dma((2, 8)), dma((2, 8)),
        dma((2, 8)), dma((2, 8)),
        dma((2, 2, 4)), dma((2, 2, 4)),
        dma((2, 2, 4)), dma((2, 2, 4)),
        dma((2, 8)), dma((2, 8)),
        dma((2, 8)), dma((2, 8)),
        dma((2, 8)), dma((2, 8)),
        dma((2, 8)), dma((2, 8)),
        dma((2, 2)), dma((2, 2)),
        dma((9,)), dma((9,)),
        dma((4,)), dma((4,)),
    ]
    return pl.pallas_call(
        kernel,
        out_shape=[shard, shard, update, update, update],
        in_specs=[in_vmem] * 5 + [in_any] * 9,
        out_specs=[in_vmem] * 2 + [in_any] * 3,
        scratch_shapes=scratch,
        compiler_params=pltpu.CompilerParams(
            collective_id=0, has_side_effects=True, vmem_limit_bytes=58 * 1024 * 1024
        ),
        cost_estimate=pl.CostEstimate(flops=5_100_000_000, bytes_accessed=12_000_000, transcendentals=1_000_000),
        name="fused_step",
    )(*inputs)


def handing_on(*refs):
    for a, b in zip(refs[:5], refs[5:]):
        b[...] = a[...]


def hand_on(*results):
    in_vmem = pl.BlockSpec(memory_space=pltpu.VMEM)
    return pl.pallas_call(
        handing_on,
        out_shape=[jax.ShapeDtypeStruct(r.shape, r.dtype) for r in results],
        in_specs=[in_vmem] * 5,
        out_specs=[in_vmem] * 5,
        name="hand_on",
    )(*results)


def body(tokens, cotangent, pass_counts, group_ids, token_rollout, *states):
    results = step(
        tokens.T,
        cotangent.T,
        pass_counts.reshape(1, ROLL),
        group_ids.reshape(1, ROLL),
        token_rollout.reshape(1, TB),
        *states,
    )
    block_out, grad_input, update_gate, update_up, update_down = hand_on(*results)
    return block_out.T, grad_input.T, update_gate, update_up, update_down


def solution(mesh):
    act, rep, weight = P("dp", "fsdp"), P(), P("fsdp", "dp")
    return jax.shard_map(
        body,
        mesh=mesh,
        in_specs=(act, act, rep, rep, P("dp")) + (weight,) * 9,
        out_specs=(act, act, weight, weight, weight),
        check_vma=False,
    )
```

time: 155 us -> 138 us (0.89)
  local copies, waits for them, and re-layouts: 6.42 us -> 0 us
  Pallas kernels: 143 us -> 137 us
  other arithmetic: 4.42 us -> 0 us
    pallas_call x1, Pallas kernels: 143 us -> 135 us  [step(): pl.pallas_call(kernel, out_shape=[shard, shard, update, update, update],...]
    unnamed x9 -> x0, local copies, waits for them, and re-layouts: 6.42 us -> none
    pallas_call x0 -> x1, Pallas kernels: none -> 2.65 us  [hand_on(): pl.pallas_call(handing_on, out_shape=[jax.ShapeDtypeStruct(r.shape, r.dty...]
    reduce_sum x2 -> x0, other arithmetic: 1.68 us -> none  [the longest x1 0.9 us: body(): jnp.sum(same_group, axis=1)]
where the time goes in v2:
time: 138 us
  Pallas kernels  137 us (99%)
    pallas_call x1, Pallas kernels, step(): pl.pallas_call(kernel, out_shape=[shard, shard, update, update, update],...  135 us

profile of v2, /device:TPU:1, one launch (start us, length us, event | category | flops | bytes accessed | tf_op | source)
XLA Modules:
  0.0 138.1 jit_solution(5725436379357923558)
XLA Ops:
  0.6 134.8 %fused_step.1 = (bf16[80,256]{1,0:T(8,128)(2,1)}, bf16[80,256]{1,0:T(8,128)(2,1)}, bf16[216,1280]{1,0:T(8,128)(2,1)}, bf16[216,1280]{1,0:T(8,128)(2,1)}, bf16[216,1280]{1,0:T(8,128)(2,1)}) custom-call(bf16[80,256]{1,0:T(8,128)(2,1)} %bitcast.7, bf16[80,256]{1,0:T(8,128)(2,1)} %bitcast.8, s32[1,64]{1,0:T(1,128)} %bitcast.12, s32[1,64]{1,0:T(1,128)} %bitcast.13, ...), custom_call_target="tpu_custom_call" | custom-call | flops 5100000256 | bytes 12000000 | tf_op jit(solution)/shard_map/fused_step/pallas_call | solution.py:702
  135.4 2.6 %hand_on.1 = (bf16[80,256]{1,0:T(8,128)(2,1)}, bf16[80,256]{1,0:T(8,128)(2,1)}, bf16[216,1280]{1,0:T(8,128)(2,1)}, bf16[216,1280]{1,0:T(8,128)(2,1)}, bf16[216,1280]{1,0:T(8,128)(2,1)}) custom-call(bf16[80,256]{1,0:T(8,128)(2,1)} %get-tuple-element.15.refs_0_, bf16[80,256]{1,0:T(8,128)(2,1)} %get-tuple-element.16.refs_1_, ...), custom_call_target="tpu_custom_call" | custom-call | tf_op jit(solution)/shard_map/hand_on/pallas_call | solution.py:723

commit v3 on v2

--- a/solution.py
+++ b/solution.py
@@ -20,6 +20,8 @@
 DS = 1280
 FB = 80
 TB = 256
+NEAR = (0, 1, 7, 2, 6, 3, 5, 4)
+FAR = (4, 3, 5, 2, 6, 1, 7, 0)
 F32 = jnp.float32
 BF16 = jnp.bfloat16
 
@@ -126,9 +128,12 @@
     def _():
         pl.semaphore_wait(barrier, 28)
 
+    def came(k):
+        return rem(z + 8 - NEAR[k], 8)
+
     def z_copy(a, n, t):
         return remote(
-            TT.at[a], XT.at[a, x, own, yh], z_s.at[a, n, t], z_r.at[a, n, yh], at(home, rem(own + n, 8), t, x)
+            TT.at[a], XT.at[a, x, own, yh], z_s.at[a, n, t], z_r.at[a, n, yh], at(home, rem(own + NEAR[n], 8), t, x)
         )
 
     def z_start(a, n):
@@ -141,12 +146,12 @@
         for s in range(2):
             @pl.when(jnp.logical_and(jnp.logical_not(is_self(k, s)), jnp.logical_or(k >= 2, s == yh)))
             def _():
-                got = XT.at[a, x, rem(z + 8 - k, 8), s]
+                got = XT.at[a, x, came(k), s]
                 remote(got, got, z_s.at[a, k, s], z_r.at[a, k, s], d_right).wait_recv()
 
     def piece(a, xx, k):
-        block = XT.at[a, xx, rem(z + 8 - k, 8)]
-        return block.at[yh] if isinstance(k, int) and k < 2 else block
+        block = XT.at[a, xx, came(k)]
+        return block.at[yh] if k < 2 else block
 
     def x_copy(a, k, to_right):
         mine = piece(a, x, k)
@@ -169,11 +174,11 @@
         return remote(got, got, f_s.at[a, k], f_r.at[a, k], d_right)
 
     def v_copy(a, k, xx):
-        mine = XT.at[a, xx, rem(z + 8 - k, 8), yh]
+        mine = XT.at[a, xx, came(k), yh]
         return remote(mine, mine, v_s.at[a, k, xx], v_r.at[a, k, xx], d_y)
 
     def v_recv(a, k, xx):
-        got = XT.at[a, xx, rem(z + 8 - k, 8), 1 - yh]
+        got = XT.at[a, xx, came(k), 1 - yh]
         return remote(got, got, v_s.at[a, k, xx], v_r.at[a, k, xx], d_y)
 
     def gather_home(a):
@@ -207,38 +212,21 @@
             x_copy(a, k, True).start()
             x_copy(a, k, False).start()
             if a == 0:
-                @pl.when(k < 5)
-                def _():
-                    z_start(0, k + 3)
-
-                @pl.when(k >= 5)
-                def _():
-                    z_start(1, k - 5)
+                z_start(1, k)
 
     def gather_x(a):
         gather_step(a, 0)
-        if a == 0:
-            v_start(0, x)
-            gather_step(a, 1)
-            forward_first(a)
-            v_start(0, left, right)
-
-            @pl.loop(2, 4)
-            def _(j):
-                gather_step(a, j)
-                forward(a, j - 1)
-
-            @pl.loop(3, 8)
-            def _(n):
-                z_start(1, n)
-        else:
-            @pl.loop(1, 4)
-            def _(j):
-                gather_step(a, j)
+        v_start(0, x)
+        gather_step(a, 1)
+        gather_step(a, 2)
+        forward_first(a)
+        v_start(0, left, right)
+        gather_step(a, 3)
+        forward(a, 1)
+        forward(a, 2)
 
     def gather_end(a):
-        @pl.loop(1, 4)
-        def _(j):
+        for j in range(1, 4):
             x_recv(a, 2 * j, False).wait_recv()
             x_recv(a, 2 * j + 1, True).wait_recv()
             f_recv(a, 2 * j).wait_recv()
@@ -264,10 +252,10 @@
                 v_copy(a, k, n).wait_send()
 
     def place(k):
-        return rem(z + k, 8)
+        return rem(z + FAR[k], 8)
 
     def late(k):
-        return isinstance(k, int) and k >= 6
+        return k >= 6
 
     def part(a, xx, k):
         block = PO.at[a, xx, place(k)]
@@ -353,31 +341,24 @@
             mine[...] = (
                 mine[...].astype(F32) + slot(RXR, a, k)[...].astype(F32) + slot(RXC, a, k)[...].astype(F32)
             ).astype(BF16)
-            if late(k):
+            if k < 7:
                 zz_copy(a, k).start()
-            else:
-                @pl.when(k > 0)
-                def _():
-                    zz_copy(a, k).start()
 
     def sum_finish(a):
-        @pl.loop(0, 3)
-        def _(j):
+        for j in range(4):
             finish(a, j)
 
-        finish(a, 3)
-
     def sum_z(a):
-        for k in range(1, 8):
+        for k in range(7):
             zz_copy(a, k).wait_recv()
         for s in range(2):
-            total = PO[a, x, z, s].astype(F32)
+            total = ZR[a, 0, s].astype(F32)
             for k in range(1, 6):
                 total = total + ZR[a, k, s].astype(F32)
 
             @pl.when(s == yh)
             def _():
-                YS[a, s] = (total + ZR[a, 6, s].astype(F32) + ZR[a, 7, s].astype(F32)).astype(BF16)
+                YS[a, s] = (total + ZR[a, 6, s].astype(F32) + PO[a, x, z, s].astype(F32)).astype(BF16)
 
             @pl.when(s != yh)
             def _():
@@ -410,7 +391,7 @@
                 o_copy(a, k, to_right).wait_send()
                 w_copy(a, k, not to_right).wait_send()
                 c_copy(a, k, to_right).wait_send()
-                if k > 0:
+                if k < 7:
                     zz_copy(a, k).wait_send()
 
         for s in range(2):
@@ -479,19 +460,18 @@
 
     gather_home(0)
 
-    @pl.loop(0, 3)
-    def _(n):
+    for n in range(8):
         z_start(0, n)
 
     gather_home(1)
-    weights(0)
-    weights(1)
     gather_x(0)
+    gather_step(1, 0)
     forward_far(0)
     v_start(0, far)
+    gather_step(1, 1)
     forward(0, 3)
-    weights(2)
-    gather_x(1)
+    for w in range(3):
+        weights(w)
     gather_end(0)
 
     @pl.loop(0, 2)
@@ -513,11 +493,10 @@
         SY[k, 1] = up.astype(BF16)
         chip_copy(k, SY.at[k], RY.at[k]).start()
 
+    gather_step(1, 2)
     forward_first(1)
-
-    @pl.loop(1, 4)
-    def _(j):
-        forward(1, j)
+    gather_step(1, 3)
+    forward(1, 1)
 
     @pl.loop(0, 2)
     def _(k):
@@ -532,8 +511,8 @@
         HD[2 * core + k, 0:PAD, :] = (active * up_in).astype(BF16)
         core_copy(1 + k, mine, mine).start()
 
-    forward_far(1)
-    v_start(1, x, left, right, far)
+    v_start(1, x, left, right)
+    forward(1, 2)
 
     @pl.loop(0, 2)
     def _(k):
@@ -544,6 +523,9 @@
     def _(tb):
         scatter_rows(0, tb, dot(WT[2], HD[tb]))
 
+    forward_far(1)
+    v_start(1, far)
+    forward(1, 3)
     sum_start(0)
     gather_end(1)
 
@@ -566,11 +548,11 @@
         chip_copy(2 + k, SY2.at[k], RY2.at[k]).start()
 
     combine(0, 0)
+    combine(0, 1)
     fold_y(0)
     o_start(0, 3)
     w_start(0, 3)
-    for j in range(1, 4):
-        combine(0, j)
+    combine(0, 2)
     grad(HD, 1)
     store_down = adamw(2, UO2, ud)
 
@@ -583,6 +565,8 @@
         DU[2 * core + k, 0:PAD, :] = (d_hidden * ACT[k]).astype(BF16)
         core_copy(4 + k, gate, gate).start()
         core_copy(6 + k, up, up).start()
+
+    combine(0, 3)
 
     @pl.loop(0, 2)
     def _(k):

time: 138 us -> 131 us (0.949)
  Pallas kernels: 137 us -> 130 us
    pallas_call x1, Pallas kernels: 135 us -> 127 us  [step(): pl.pallas_call(kernel, out_shape=[shard, shard, update, update, update],...]
where the time goes in v3:
time: 131 us; the launch traced here: 130 us
  Pallas kernels  130 us (99%)
    pallas_call x1, Pallas kernels, step(): pl.pallas_call(kernel, out_shape=[shard, shard, update, update, update],...  127 us
    pallas_call x1, Pallas kernels, hand_on(): pl.pallas_call(handing_on, out_shape=[jax.ShapeDtypeStruct(r.shape, r.dty...  2.65 us

profile of v3, /device:TPU:1, one launch (start us, length us, event | category | flops | bytes accessed | tf_op | source)
XLA Modules:
  0.0 130.4 jit_solution(8539525295953163950)
XLA Ops:
  0.6 127.1 %fused_step.1 = (bf16[80,256]{1,0:T(8,128)(2,1)}, bf16[80,256]{1,0:T(8,128)(2,1)}, bf16[216,1280]{1,0:T(8,128)(2,1)}, bf16[216,1280]{1,0:T(8,128)(2,1)}, bf16[216,1280]{1,0:T(8,128)(2,1)}) custom-call(bf16[80,256]{1,0:T(8,128)(2,1)} %bitcast.7, bf16[80,256]{1,0:T(8,128)(2,1)} %bitcast.8, s32[1,64]{1,0:T(1,128)} %bitcast.12, s32[1,64]{1,0:T(1,128)} %bitcast.13, ...), custom_call_target="tpu_custom_call" | custom-call | flops 5100000256 | bytes 12000000 | tf_op jit(solution)/shard_map/fused_step/pallas_call | solution.py:686
  127.8 2.6 %hand_on.1 = (bf16[80,256]{1,0:T(8,128)(2,1)}, bf16[80,256]{1,0:T(8,128)(2,1)}, bf16[216,1280]{1,0:T(8,128)(2,1)}, bf16[216,1280]{1,0:T(8,128)(2,1)}, bf16[216,1280]{1,0:T(8,128)(2,1)}) custom-call(bf16[80,256]{1,0:T(8,128)(2,1)} %get-tuple-element.15.refs_0_, bf16[80,256]{1,0:T(8,128)(2,1)} %get-tuple-element.16.refs_1_, ...), custom_call_target="tpu_custom_call" | custom-call | tf_op jit(solution)/shard_map/hand_on/pallas_call | solution.py:707

commit v4 on v3

--- a/solution.py
+++ b/solution.py
@@ -48,7 +48,7 @@
 def kernel(
     tok, cot, counts, groups, rolls, mg, mu, md, og, ou, od, sg, su, sd,
     bo, gi, ug, uu, ud,
-    TT, XT, PO, RV, RXO, RXR, RXC, ZR, YS, FR,
+    TT, COT, CN, GP, RL, XT, PO, RV, RXO, RXR, RXC, ZR, YS, FR,
     MW, MOM, SEC, WB, WT, HD, DG, DU, GUO, ACT, US, DHO,
     SD, RD, SY, RY, SD2, RD2, SY2, RY2, GR, UO0, UO1, UO2,
     lsem, z_s, z_r, xr_s, xr_r, xl_s, xl_r, f_s, f_r,
@@ -72,6 +72,33 @@
     d_core = at(dp + 1 - 2 * core, z, yh, x)
     d_chip = at(rem(dp + 2, 4), z, yh, x)
 
+    def is_self(n, t):
+        return jnp.logical_and(jnp.logical_and(at_home, n == 0), t == yh)
+
+    barrier = pltpu.get_barrier_semaphore()
+
+    def greet(peer):
+        pl.semaphore_signal(barrier, inc=1, device_id=peer, device_id_type=pl.DeviceIdType.MESH)
+
+    for peer in (d_right, d_left, d_core, d_chip, d_y):
+        greet(peer)
+
+    @pl.loop(1, 8)
+    def _(n):
+        greet(at(dp, rem(z + n, 8), yh, x))
+
+    @pl.loop(0, 8)
+    def _(n):
+        for t in range(2):
+            @pl.when(jnp.logical_not(is_self(n, t)))
+            def _():
+                greet(at(div(rem(z + n, 8), 2), 2 * dp + rem(z + n, 2), t, x))
+
+    smalls = []
+    for n, (src, dst) in enumerate(zip((tok, cot, counts, groups, rolls), (TT.at[0], COT, CN, GP, RL))):
+        smalls.append(pltpu.make_async_copy(src, dst, lsem.at[12 + n]))
+    for small in smalls:
+        small.start()
     srcs = (mg, mu, md, og, ou, od, sg, su, sd)
     loads = []
     for n, src in enumerate(srcs):
@@ -83,42 +110,22 @@
     for w in range(3):
         MW[w, FFS:HID, :] = jnp.zeros((HID - FFS, DS), F32)
     for buf in (HD, DG, DU):
-        for n in range(4):
-            buf[n, PAD:HID, :] = jnp.zeros((HID - PAD, TB), BF16)
-
-    def is_self(n, t):
-        return jnp.logical_and(jnp.logical_and(at_home, n == 0), t == yh)
-
-    barrier = pltpu.get_barrier_semaphore()
-
-    def greet(peer):
-        pl.semaphore_signal(barrier, inc=1, device_id=peer, device_id_type=pl.DeviceIdType.MESH)
-
-    for peer in (d_right, d_left, d_core, d_chip, d_y):
-        greet(peer)
-
-    @pl.loop(1, 8)
-    def _(n):
-        greet(at(dp, rem(z + n, 8), yh, x))
-
-    @pl.loop(0, 8)
-    def _(n):
-        for t in range(2):
-            @pl.when(jnp.logical_not(is_self(n, t)))
-            def _():
-                greet(at(div(rem(z + n, 8), 2), 2 * dp + rem(z + n, 2), t, x))
-
-    reward = counts[...].astype(F32) / TESTS
-    group = groups[...].astype(F32)
+        for n in range(2):
+            buf[2 * core + n, PAD:HID, :] = jnp.zeros((HID - PAD, TB), BF16)
+
+    for small in smalls:
+        small.wait()
+
+    reward = CN[...].astype(F32) / TESTS
+    group = GP[...].astype(F32)
     group_col = jnp.broadcast_to(group, (ROLL, ROLL)).T
     same = (group_col == group).astype(F32)
     baseline = jnp.sum(same * reward, axis=1, keepdims=True) / jnp.sum(same, axis=1, keepdims=True)
     reward_col = jnp.broadcast_to(reward, (ROLL, ROLL)).T[:, 0:1]
     advantage = reward_col - baseline
     rollout = lax.broadcasted_iota(jnp.int32, (ROLL, TB), 0)
-    token_adv = jnp.sum(jnp.where(rollout == rolls[...], advantage, 0.0), axis=0, keepdims=True)
-    TT[0] = tok[...]
-    TT[1] = (-token_adv * cot[...].astype(F32)).astype(BF16)
+    token_adv = jnp.sum(jnp.where(rollout == RL[...], advantage, 0.0), axis=0, keepdims=True)
+    TT[1] = (-token_adv * COT[...].astype(F32)).astype(BF16)
 
     @pl.when(at_home)
     def _():
@@ -635,6 +642,10 @@
     in_any = pl.BlockSpec(memory_space=pl.ANY)
     scratch = [
         vmem(2, FB, TB),
+        vmem(FB, TB),
+        vmem(1, ROLL, dtype=jnp.int32),
+        vmem(1, ROLL, dtype=jnp.int32),
+        vmem(1, TB, dtype=jnp.int32),
         vmem(2, 4, 8, 2, FB, TB),
         vmem(2, 4, 8, 2, FB, TB),
         vmem(2, 2, 4, FB, TB),
@@ -668,7 +679,7 @@
         vmem(FFS, DS),
         vmem(FFS, DS),
         vmem(FFS, DS),
-        dma((12,)),
+        dma((17,)),
         dma((2, 8, 2)), dma((2, 8, 2)),
         dma((2, 8)), dma((2, 8)),
         dma((2, 8)), dma((2, 8)),
@@ -686,7 +697,7 @@
     return pl.pallas_call(
         kernel,
         out_shape=[shard, shard, update, update, update],
-        in_specs=[in_vmem] * 5 + [in_any] * 9,
+        in_specs=[in_any] * 14,
         out_specs=[in_vmem] * 2 + [in_any] * 3,
         scratch_shapes=scratch,
         compiler_params=pltpu.CompilerParams(

time: 131 us -> 130 us (level)
  no operation moved by 1% of the time
where the time goes in v4:
time: 130 us; the launch traced here: 129 us
  Pallas kernels  129 us (99%)
    pallas_call x1, Pallas kernels, step(): pl.pallas_call(kernel, out_shape=[shard, shard, update, update, update],...  126 us
    pallas_call x1, Pallas kernels, hand_on(): pl.pallas_call(handing_on, out_shape=[jax.ShapeDtypeStruct(r.shape, r.dty...  2.65 us

profile of v4, /device:TPU:1, one launch (start us, length us, event | category | flops | bytes accessed | tf_op | source)
XLA Modules:
  0.0 129.5 jit_solution(13742077826011633330)
XLA Ops:
  0.6 126.2 %fused_step.1 = (bf16[80,256]{1,0:T(8,128)(2,1)}, bf16[80,256]{1,0:T(8,128)(2,1)}, bf16[216,1280]{1,0:T(8,128)(2,1)}, bf16[216,1280]{1,0:T(8,128)(2,1)}, bf16[216,1280]{1,0:T(8,128)(2,1)}) custom-call(bf16[80,256]{1,0:T(8,128)(2,1)} %bitcast.7, bf16[80,256]{1,0:T(8,128)(2,1)} %bitcast.8, s32[1,64]{1,0:T(1,128)} %bitcast.12, s32[1,64]{1,0:T(1,128)} %bitcast.13, ...), custom_call_target="tpu_custom_call" | custom-call | flops 5100000256 | bytes 12000000 | tf_op jit(solution)/shard_map/fused_step/pallas_call | solution.py:697
  126.8 2.6 %hand_on.1 = (bf16[80,256]{1,0:T(8,128)(2,1)}, bf16[80,256]{1,0:T(8,128)(2,1)}, bf16[216,1280]{1,0:T(8,128)(2,1)}, bf16[216,1280]{1,0:T(8,128)(2,1)}, bf16[216,1280]{1,0:T(8,128)(2,1)}) custom-call(bf16[80,256]{1,0:T(8,128)(2,1)} %get-tuple-element.15.refs_0_, bf16[80,256]{1,0:T(8,128)(2,1)} %get-tuple-element.16.refs_1_, ...), custom_call_target="tpu_custom_call" | custom-call | tf_op jit(solution)/shard_map/hand_on/pallas_call | solution.py:718

commit v5 on v4

--- a/solution.py
+++ b/solution.py
@@ -477,8 +477,8 @@
     v_start(0, far)
     gather_step(1, 1)
     forward(0, 3)
-    for w in range(3):
-        weights(w)
+    weights(0)
+    weights(1)
     gather_end(0)
 
     @pl.loop(0, 2)
@@ -501,6 +501,7 @@
         chip_copy(k, SY.at[k], RY.at[k]).start()
 
     gather_step(1, 2)
+    weights(2)
     forward_first(1)
     gather_step(1, 3)
     forward(1, 1)
@@ -709,17 +710,27 @@
 
 
 def handing_on(*refs):
-    for a, b in zip(refs[:5], refs[5:]):
-        b[...] = a[...]
+    arrays, results, held, sems = refs[:5], refs[5:10], refs[10:15], refs[15]
+    fetches = [pltpu.make_async_copy(a, h, sems.at[0, n]) for n, (a, h) in enumerate(zip(arrays, held))]
+    stores = [pltpu.make_async_copy(h, r, sems.at[1, n]) for n, (h, r) in enumerate(zip(held, results))]
+    for fetch in fetches:
+        fetch.start()
+    for fetch, store in zip(fetches, stores):
+        fetch.wait()
+        store.start()
+    for store in stores:
+        store.wait()
 
 
 def hand_on(*results):
-    in_vmem = pl.BlockSpec(memory_space=pltpu.VMEM)
+    in_any = pl.BlockSpec(memory_space=pl.ANY)
     return pl.pallas_call(
         handing_on,
         out_shape=[jax.ShapeDtypeStruct(r.shape, r.dtype) for r in results],
-        in_specs=[in_vmem] * 5,
-        out_specs=[in_vmem] * 5,
+        in_specs=[in_any] * 5,
+        out_specs=[in_any] * 5,
+        scratch_shapes=[pltpu.VMEM(r.shape, r.dtype) for r in results] + [pltpu.SemaphoreType.DMA((2, 5))],
+        compiler_params=pltpu.CompilerParams(vmem_limit_bytes=58 * 1024 * 1024),
         name="hand_on",
     )(*results)
 

time: 130 us -> 130 us (level)
  no operation moved by 1% of the time
where the time goes in v5:
time: 130 us; the launch traced here: 129 us
  Pallas kernels  129 us (99%)
    pallas_call x1, Pallas kernels, step(): pl.pallas_call(kernel, out_shape=[shard, shard, update, update, update],...  126 us

profile of v5, /device:TPU:1, one launch (start us, length us, event | category | flops | bytes accessed | tf_op | source)
XLA Modules:
  0.0 129.2 jit_solution(6733360053790793921)
XLA Ops:
  0.6 126.2 %fused_step.1 = (bf16[80,256]{1,0:T(8,128)(2,1)}, bf16[80,256]{1,0:T(8,128)(2,1)}, bf16[216,1280]{1,0:T(8,128)(2,1)}, bf16[216,1280]{1,0:T(8,128)(2,1)}, bf16[216,1280]{1,0:T(8,128)(2,1)}) custom-call(bf16[80,256]{1,0:T(8,128)(2,1)} %bitcast.7, bf16[80,256]{1,0:T(8,128)(2,1)} %bitcast.8, s32[1,64]{1,0:T(1,128)} %bitcast.12, s32[1,64]{1,0:T(1,128)} %bitcast.13, ...), custom_call_target="tpu_custom_call" | custom-call | flops 5100000256 | bytes 12000000 | tf_op jit(solution)/shard_map/fused_step/pallas_call | solution.py:698
  126.8 2.4 %hand_on.1 = (bf16[80,256]{1,0:T(8,128)(2,1)}, bf16[80,256]{1,0:T(8,128)(2,1)}, bf16[216,1280]{1,0:T(8,128)(2,1)}, bf16[216,1280]{1,0:T(8,128)(2,1)}, bf16[216,1280]{1,0:T(8,128)(2,1)}) custom-call(bf16[80,256]{1,0:T(8,128)(2,1)} %get-tuple-element.15.refs_0_, bf16[80,256]{1,0:T(8,128)(2,1)} %get-tuple-element.16.refs_1_, ...), custom_call_target="tpu_custom_call" | custom-call | tf_op jit(solution)/shard_map/hand_on/pallas_call | solution.py:727
